TPU v7x, 256 devices: a whole 4x4x8 slice. The times are simulated.
256 devices in a mesh: fsdp: 16 (over x_lo, y, core), seq: 16 (over x_hi, z).
Axes of the slice: x: 4 (x_hi: 2, x_lo: 2; x = x_hi * 2 + x_lo), y: 4, z: 8, core: 2. Of those that a mesh axis runs over, the one named last changes fastest.
Arguments:
- attn_inputs: bfloat16 [16, 2048, 3, 2048], P('fsdp', 'seq'), may hold values from -32 to 32
- out_weight: bfloat16 [2048, 3072], P('fsdp'), may hold values from -0.125 to 0.125
- skew_params: float32 [96, 128, 128], P('fsdp'), may hold values from -0.3 to 0.3
- piece_orders: int32 [4, 96], replicated, may hold values from 0 to 95, each once within a row
- cotangent: bfloat16 [16, 2048, 3072], P('fsdp', 'seq'), may hold values from -6 to 6
Outputs:
- block_output: bfloat16 [16, 2048, 3072], P('fsdp', 'seq')
- grad_inputs: bfloat16 [16, 2048, 3, 2048], P('fsdp', 'seq')
- grad_skew: float32 [96, 128, 128], P('fsdp')
Inputs may be any that keep to these rules, and one draw needn't show every extreme that they name: `piece_orders`: each row lists every piece number from 0 to 95 exactly once.
All inputs are finite; a program needn't handle non-finite values.
Results may differ from a plain program's by a relative error of at most 0.03.
Values may be sent and summed in bfloat16 or wider, within the bound.
No kernel may reach another device: no remote copies, remote signals or barrier semaphores. Data moves between devices by JAX's collectives and lax.ppermute only.
A program may use at most 128 MiB of HBM per device.

v0:
```python
import math
import jax
import jax.numpy as jnp
from jax import lax
from jax.sharding import PartitionSpec as P

HEADS = 16
HD = 128
BS = 128
FACTORS = 4


def cayley(skew_params):
    skewed = skew_params - jnp.swapaxes(skew_params, -1, -2)
    identity = jnp.eye(skew_params.shape[-1], dtype=skew_params.dtype)
    minus_part = identity - skewed
    gram_matrix = identity + jnp.matmul(
        jnp.swapaxes(skewed, -1, -2), skewed, precision=lax.Precision.HIGHEST
    )
    factor_low = jnp.linalg.cholesky(gram_matrix)
    halfway = lax.linalg.triangular_solve(factor_low, minus_part, left_side=True, lower=True)
    solved = lax.linalg.triangular_solve(
        factor_low, halfway, left_side=True, lower=True, transpose_a=True
    )
    return jnp.matmul(minus_part, solved, precision=lax.Precision.HIGHEST)


def reorder(matrix, ordering):
    row_count = matrix.shape[0]
    return jnp.take(matrix.reshape(row_count, ordering.shape[0], -1), ordering, axis=1).reshape(
        row_count, -1
    )


def inverse_order(ordering):
    return jnp.zeros_like(ordering).at[ordering].set(jnp.arange(ordering.shape[0], dtype=jnp.int32))


def local(attn_inputs, out_weight, skew_params, piece_orders, cotangent):
    seq_count = lax.axis_size("seq")
    tok_count = attn_inputs.shape[1]
    full_width = attn_inputs.shape[3]
    model_width = out_weight.shape[1]
    heads_here = HEADS // seq_count
    group_width = heads_here * HD
    length_all = tok_count * seq_count
    scaling = 1.0 / math.sqrt(HD)
    blocks_per = model_width // BS
    weight_full = lax.all_gather(out_weight, "fsdp", axis=0, tiled=True)
    rot_own = cayley(skew_params).astype(jnp.bfloat16)
    rotations = lax.all_gather(rot_own, "fsdp", axis=0, tiled=True).reshape(
        FACTORS, blocks_per, BS, BS
    )
    local_rows = attn_inputs[0].reshape(tok_count, 3, seq_count, group_width)
    spread = lax.all_to_all(local_rows, "seq", split_axis=2, concat_axis=0, tiled=True)
    queries = spread[:, 0]
    key_rows = spread[:, 1]
    value_rows = spread[:, 2]
    block_rows = min(512, length_all)
    block_count = length_all // block_rows
    query_blocks = queries.reshape(block_count, block_rows, heads_here, HD)

    def forward_block(query_block):
        scores = (
            jnp.einsum("qhd,khd->hqk", query_block, key_rows, preferred_element_type=jnp.float32)
            * scaling
        )
        shifted = jnp.exp(scores - jnp.max(scores, axis=-1, keepdims=True))
        rounded = (shifted / jnp.sum(shifted, axis=-1, keepdims=True)).astype(jnp.bfloat16)
        wide_out = jnp.einsum(
            "hqk,khd->qhd", rounded, value_rows, preferred_element_type=jnp.float32
        )
        return (wide_out.astype(jnp.bfloat16), wide_out, rounded)

    attended, wide_blocks, rounded_blocks = lax.map(forward_block, query_blocks)
    attended = attended.reshape(length_all, 1, group_width)
    attended = lax.all_to_all(attended, "seq", split_axis=0, concat_axis=1, tiled=True).reshape(
        tok_count, full_width
    )
    projected = jnp.dot(attended, weight_full, preferred_element_type=jnp.float32).astype(
        jnp.bfloat16
    )
    current = projected
    saved_rows = []
    for factor in range(FACTORS):
        ordering = piece_orders[factor]
        moved_rows = reorder(current, ordering).reshape(tok_count, blocks_per, BS)
        saved_rows.append(moved_rows)
        mixed_rows = jnp.einsum(
            "tjb,jbc->tjc", moved_rows, rotations[factor], preferred_element_type=jnp.float32
        )
        current = reorder(
            mixed_rows.reshape(tok_count, model_width), inverse_order(ordering)
        ).astype(jnp.bfloat16)
    block_output = current.reshape(1, tok_count, model_width)
    upstream = cotangent[0]
    pieces_grad = [None] * FACTORS
    for factor in reversed(range(FACTORS)):
        ordering = piece_orders[factor]
        moved_grad = reorder(upstream, ordering).reshape(tok_count, blocks_per, BS)
        pieces_grad[factor] = jnp.einsum(
            "tjb,tjc->jbc", saved_rows[factor], moved_grad, preferred_element_type=jnp.float32
        )
        back_mixed = jnp.einsum(
            "tjc,jbc->tjb", moved_grad, rotations[factor], preferred_element_type=jnp.float32
        )
        upstream = reorder(
            back_mixed.reshape(tok_count, model_width), inverse_order(ordering)
        ).astype(jnp.bfloat16)
    rot_grad = jnp.stack(pieces_grad).reshape(FACTORS * blocks_per, BS, BS)
    grad_attended = lax.dot_general(
        upstream, weight_full, (((1,), (1,)), ((), ())), preferred_element_type=jnp.float32
    ).astype(jnp.bfloat16)
    grad_spread = lax.all_to_all(
        grad_attended.reshape(tok_count, seq_count, group_width),
        "seq",
        split_axis=1,
        concat_axis=0,
        tiled=True,
    )
    grad_spread = grad_spread.reshape(block_count, block_rows, heads_here, HD)

    def backward_block(carry, items):
        key_acc, value_acc = carry
        query_block, dout_block, rounded, wide_out = items
        dprobs = jnp.einsum(
            "qhd,khd->hqk", dout_block, value_rows, preferred_element_type=jnp.float32
        )
        centre = jnp.einsum("qhd,qhd->hq", dout_block.astype(jnp.float32), wide_out)[:, :, None]
        dscores = (rounded.astype(jnp.float32) * (dprobs - centre) * scaling).astype(jnp.bfloat16)
        grad_q = jnp.einsum(
            "hqk,khd->qhd", dscores, key_rows, preferred_element_type=jnp.float32
        ).astype(jnp.bfloat16)
        key_acc = key_acc + jnp.einsum(
            "hqk,qhd->khd", dscores, query_block, preferred_element_type=jnp.float32
        )
        value_acc = value_acc + jnp.einsum(
            "hqk,qhd->khd", rounded, dout_block, preferred_element_type=jnp.float32
        )
        return ((key_acc, value_acc), grad_q)

    zero_acc = jnp.zeros((length_all, heads_here, HD), jnp.float32)
    (key_acc, value_acc), query_grads = lax.scan(
        backward_block,
        (zero_acc, zero_acc),
        (query_blocks, grad_spread, rounded_blocks, wide_blocks),
    )
    stacked = jnp.stack(
        [
            query_grads.reshape(length_all, group_width),
            key_acc.astype(jnp.bfloat16).reshape(length_all, group_width),
            value_acc.astype(jnp.bfloat16).reshape(length_all, group_width),
        ],
        axis=1,
    )
    stacked = stacked.reshape(length_all, 3, 1, group_width)
    grad_inputs = lax.all_to_all(stacked, "seq", split_axis=0, concat_axis=2, tiled=True).reshape(
        1, tok_count, 3, full_width
    )
    block_share = lax.psum_scatter(
        rot_grad.astype(jnp.bfloat16), "fsdp", scatter_dimension=0, tiled=True
    )
    owner_grad = lax.psum(block_share, "seq").astype(jnp.float32)
    total_tokens = lax.axis_size("fsdp") * length_all
    unused, pullback = jax.vjp(cayley, skew_params)
    grad_skew = pullback(owner_grad * (1.0 / math.sqrt(total_tokens)))[0]
    return (block_output, grad_inputs, grad_skew)


def solution(mesh):
    in_specs = (
        P("fsdp", "seq", None, None),
        P("fsdp", None),
        P("fsdp", None, None),
        P(),
        P("fsdp", "seq", None),
    )
    out_specs = (P("fsdp", "seq", None), P("fsdp", "seq", None, None), P("fsdp", None, None))
    return jax.shard_map(local, mesh=mesh, in_specs=in_specs, out_specs=out_specs, check_vma=False)
```

profile of v0, /device:TPU:2, one launch (start us, length us, event | category | flops | bytes accessed | tf_op | source)
XLA Modules:
  0.0 698.2 jit_solution(13345446725951341136)
XLA Ops:
  10.6 70.3 %custom-call.23 = f32[6,128,128]{2,1,0:T(8,128)S(1)} custom-call(f32[6,128,128]{2,1,0:T(8,128)S(1)} %fusion.64), custom_call_target="Cholesky" | custom-call | tf_op jit(solution)/shard_map/jit(cholesky)/cholesky/custom-call.1 | solution.py:20
  82.6 58.9 %custom-call.25 = f32[6,1,128,128]{2,3,1,0:T(8,128)S(1)} custom-call(f32[6,1,128,128]{3,2,1,0:T(8,128)S(1)} %get-tuple-element.302), custom_call_target="InvertDiagBlocksLowerTriangular" | custom-call | tf_op jit(solution)/shard_map/triangular_solve/custom-call.0 | solution.py:22
  147.5 10.1 %all-to-all-start = ((bf16[128,3,16,128]{3,0,1,2:T(8,128)(2,1)}), bf16[128,3,16,128]{3,0,1,2:T(8,128)(2,1)S(1)}, u32[]{:S(2)}, u32[]{:S(2)}) async-start(bf16[128,3,16,128]{3,0,1,2:T(8,128)(2,1)} %copy.274), calls=%async_computation | async-start | bytes 3145728 | tf_op jit(solution)/shard_map/all_to_all | solution.py:55
  161.6 35.6 %all-to-all-done = bf16[128,3,16,128]{3,0,1,2:T(8,128)(2,1)S(1)} async-done(((bf16[128,3,16,128]{3,0,1,2:T(8,128)(2,1)}), bf16[128,3,16,128]{3,0,1,2:T(8,128)(2,1)S(1)}, u32[]{:S(2)}, u32[]{:S(2)}) %all-to-all-start) | async-done | bytes 1572896 | tf_op jit(solution)/shard_map/all_to_all | solution.py:55
  197.6 21.2 %while.29 = (s32[]{:T(128)}, bf16[4,512,1,128]{3,1,2,0:T(8,128)(2,1)S(1)}, f32[4,512,1,128]{3,1,2,0:T(8,128)}, bf16[4,1,512,2048]{3,2,1,0:T(8,128)(2,1)}, bf16[4...) while((s32[]{:T(128)}, ...), condition=%wide.region_5.9_spmd, body=%wide.region_2.8_spmd.sunk | while | flops 546372608 | bytes 20982876 | solution.py:75
  221.6 4.9 all-to-all-start.1
  227.8 15.7 %all-to-all-done.1 = bf16[16,2,8192]{2,1,0:T(2,128)(2,1)S(1)} async-done(((bf16[16,2,8192]{2,1,0:T(2,128)(2,1)}), bf16[16,2,8192]{2,1,0:T(2,128)(2,1)S(1)}, u32[]{:S(2)}, u32[]{:S(2)}) %all-to-all-start.1) | async-done | bytes 524320 | tf_op jit(solution)/shard_map/all_to_all | solution.py:77
  248.6 2.9 gather_fusion.10
  254.0 2.7 gather_fusion.11
  259.0 2.7 gather_fusion.12
  264.3 2.7 gather_fusion.13
  269.3 2.7 gather_fusion.14
  272.0 7.0 %all-gather.5.cloned.1.call-done = bf16[2048,3072]{1,0:T(8,128)(2,1)} async-done(((bf16[128,3072]{1,0:T(8,128)(2,1)}), bf16[2048,3072]{1,0:T(8,128)(2,1)}) %all-gather.5.cloned.1.call-update) | async-done | bytes 12582928 | tf_op jit(solution)/shard_map/all_gather | solution.py:49
  279.0 7.5 %convolution_convert_fusion.1 = bf16[128,3072]{1,0:T(8,128)(2,1)} fusion(bf16[128,2048]{0,1:T(8,128)(2,1)} %bitcast.438, bf16[2048,3072]{1,0:T(8,128)(2,1)} %all-gather.5.cloned.1.call-done), kind=kOutput, calls=%fused_computation.60 | convolution fusion | flops 1611005952 | bytes 13893632 | tf_op jit(solution)/shard_map/dot_general | solution.py:80
  288.8 2.7 gather_fusion
  296.0 2.7 gather_fusion.1
  298.7 2.4 fusion.112
  301.1 2.7 gather_fusion.15
  303.8 2.9 bitcast_convert_fusion.1
  306.7 2.7 gather_fusion.2
  312.1 2.7 gather_fusion.3
  317.1 2.7 gather_fusion.4
  322.4 2.7 gather_fusion.5
  327.4 17.7 %fusion.32 = bf16[16,16,8,128]{3,2,1,0:T(8,128)(2,1)S(1)} fusion(bf16[128,3072]{0,1:T(8,128)(2,1)} %bitcast.437, bf16[2048,3072]{1,0:T(8,128)(2,1)} %all-gather.5.cloned.1.call-done), kind=kOutput, calls=%fused_computation.80 | convolution fusion | flops 1610874880 | bytes 13893632 | tf_op jit(solution)/shard_map/dot_general | solution.py:111
  346.1 9.2 %all-to-all-start.2 = ((bf16[128,16,128]{2,0,1:T(8,128)(2,1)}), bf16[128,16,128]{2,0,1:T(8,128)(2,1)}, u32[]{:S(2)}, u32[]{:S(2)}) async-start(bf16[128,16,128]{2,0,1:T(8,128)(2,1)} %bitcast.440), calls=%async_computation.2 | async-start | bytes 1048576 | tf_op jit(solution)/shard_map/all_to_all | solution.py:114
  355.4 2.9 fusion.29
  358.3 2.7 gather_fusion.6
  368.0 4.7 copy.307
  373.7 57.2 %while.30 = (s32[]{:T(128)}, f32[2048,1,128]{0,2,1:T(8,128)}, f32[2048,1,128]{0,2,1:T(8,128)}, bf16[4,512,1,128]{3,1,2,0:T(8,128)(2,1)}, bf16[4,512,1,128]{3,1,2...) while((s32[]{:T(128)}, f32[2048,1,128]{0,2,1:T(8,128)}, ...), condition=%wide.region_11.17_spmd.clone, body=%wide.region_10.16_spmd.clone.sunk | while | flops 1080294912 | bytes 27663552 | solution.py:143
  375.7 3.9 multiply_convert_fusion.2
  379.6 3.2 fusion.189
  384.3 3.2 fusion.190
  389.5 3.9 multiply_convert_fusion.2
  393.5 3.6 fusion.189
  398.4 3.5 fusion.190
  404.0 4.0 multiply_convert_fusion.2
  407.9 3.6 fusion.189
  412.9 3.5 fusion.190
  418.4 4.0 multiply_convert_fusion.2
  422.4 3.6 fusion.189
  427.3 3.5 fusion.190
  436.9 10.7 %copy.299 = bf16[2048,3,1,128]{3,1,2,0:T(4,128)(2,1)} copy(bf16[2048,3,1,128]{3,0,1,2:T(8,128)(2,1)S(1)} %maximum_bitcast_fusion) | data formatting | bytes 3145728 | tf_op jit(solution)/shard_map/reshape | solution.py:156
  447.6 9.6 %all-to-all-start.3 = ((bf16[2048,3,1,128]{3,1,2,0:T(4,128)(2,1)}), bf16[2048,3,1,128]{3,1,2,0:T(4,128)(2,1)}, u32[]{:S(2)}, u32[]{:S(2)}) async-start(bf16[2048,3,1,128]{3,1,2,0:T(4,128)(2,1)} %copy.299), calls=%async_computation.3 | async-start | bytes 4194304 | tf_op jit(solution)/shard_map/all_to_all | solution.py:157
  457.3 60.6 %custom-call.28 = f32[6,1,128,128]{2,3,1,0:T(8,128)} custom-call(f32[6,1,128,128]{3,2,1,0:T(8,128)} %get-tuple-element.301), custom_call_target="InvertDiagBlocksLowerTriangular" | custom-call | tf_op jit(solution)/shard_map/transpose(jvp())/triangular_solve/custom-call.3 | solution.py:22
  521.7 2.3 fusion.52
  524.1 2.4 fusion.108
  529.8 2.9 copy.300
  535.1 144.1 %all-reduce.2.cloned.1.call-done = bf16[6,128,128]{1,2,0:T(8,128)(2,1)} async-done(((bf16[6,128,128]{1,2,0:T(8,128)(2,1)}), bf16[6,128,128]{1,2,0:T(8,128)(2,1)}) %all-reduce.2.cloned.1.call-update) | async-done | bytes 196624 | tf_op jit(solution)/shard_map/psum | solution.py:163
  (242 shorter events, 121.2 us)
Async XLA Ops:
  7.2 238.0 %all-gather.3.cloned.1.call-start = ((), (), s32[]{:S(2)}) async-start(), calls=%async_computation.5 | async-start | bytes 3342336 | tf_op jit(solution)/shard_map/all_gather | solution.py:51
  7.2 135.7 %copy-start.24 = (f32[128,128]{1,0:T(8,128)}, f32[128,128]{1,0:T(8,128)S(1)}, u32[]{:S(2)}) copy-start(f32[128,128]{1,0:T(8,128)S(1)} %get-tuple-element.320) | copy-start | bytes 196612
  9.5 133.5 %copy-start.3 = (f32[6,128,128]{2,1,0:T(8,128)}, f32[6,128,128]{2,1,0:T(8,128)S(1)}, u32[]{:S(2)}) copy-start(f32[6,128,128]{2,1,0:T(8,128)S(1)} %bitcast_subtract_fusion) | copy-start | bytes 1179652
  10.5 134.4 %copy-start.25 = (bf16[1,128,3,2048]{3,1,2,0:T(8,128)(2,1)S(1)}, bf16[1,128,3,2048]{3,1,2,0:T(8,128)(2,1)}, u32[]{:S(2)}) copy-start(bf16[1,128,3,2048]{3,1,2,0:T(8,128)(2,1)} %param.18) | copy-start | bytes 4718596
  80.9 1.8 copy-start.26
  81.1 63.2 %copy-start.37 = (pred[6]{0:T(512)(128)(4,1)}, pred[6]{0:T(512)(128)(4,1)S(1)}, u32[]{:S(2)}) copy-start(pred[6]{0:T(512)(128)(4,1)S(1)} %compare_reduce_fusion) | copy-start | bytes 22
  141.6 2.7 copy-start.17
  144.2 134.8 %all-gather.5.cloned.1.call-start = ((), (), s32[]{:S(2)}) async-start(), calls=%async_computation.6 | async-start | bytes 13369344 | tf_op jit(solution)/shard_map/all_gather | solution.py:49
  145.9 11.7 %copy-start.36 = (s32[4,96]{1,0:T(4,128)S(1)}, s32[4,96]{1,0:T(4,128)}, u32[]{:S(2)}) copy-start(s32[4,96]{1,0:T(4,128)} %param.21) | copy-start | bytes 4612
  147.5 49.7 %all-to-all-start = ((bf16[128,3,16,128]{3,0,1,2:T(8,128)(2,1)}), bf16[128,3,16,128]{3,0,1,2:T(8,128)(2,1)S(1)}, u32[]{:S(2)}, u32[]{:S(2)}) async-start(bf16[128,3,16,128]{3,0,1,2:T(8,128)(2,1)} %copy.274), calls=%async_computation | async-start | bytes 3145728 | tf_op jit(solution)/shard_map/all_to_all | solution.py:55
  218.8 7.7 %copy-start.16 = (bf16[4,512,1,128]{3,1,2,0:T(8,128)(2,1)}, bf16[4,512,1,128]{3,1,2,0:T(8,128)(2,1)S(1)}, u32[]{:S(2)}) copy-start(bf16[4,512,1,128]{3,1,2,0:T(8,128)(2,1)S(1)} %get-tuple-element.514) | copy-start | bytes 1572868
  218.8 8.1 %copy-start.5 = (bf16[2048,1,128]{2,0,1:T(8,128)(2,1)}, bf16[2048,1,128]{2,0,1:T(8,128)(2,1)S(1)}, u32[]{:S(2)}) copy-start(bf16[2048,1,128]{2,0,1:T(8,128)(2,1)S(1)} %get-tuple-element.509) | copy-start | bytes 1572868
  218.8 8.8 %copy-start.2 = (bf16[2048,1,128]{2,0,1:T(8,128)(2,1)}, bf16[2048,1,128]{2,0,1:T(8,128)(2,1)S(1)}, u32[]{:S(2)}) copy-start(bf16[2048,1,128]{2,0,1:T(8,128)(2,1)S(1)} %get-tuple-element.508) | copy-start | bytes 1572868
  218.8 7.7 %copy-start.28 = (bf16[1,128,3072]{2,1,0:T(8,128)(2,1)S(1)}, bf16[1,128,3072]{2,1,0:T(8,128)(2,1)}, u32[]{:S(2)}) copy-start(bf16[1,128,3072]{2,1,0:T(8,128)(2,1)} %param.22) | copy-start | bytes 2359300
  221.6 22.0 %all-to-all-start.1 = ((bf16[16,2,8192]{2,1,0:T(2,128)(2,1)}), bf16[16,2,8192]{2,1,0:T(2,128)(2,1)S(1)}, u32[]{:S(2)}, u32[]{:S(2)}) async-start(bf16[16,2,8192]{2,1,0:T(2,128)(2,1)} %reshape.569), calls=%async_computation.1 | async-start | bytes 1048576 | tf_op jit(solution)/shard_map/all_to_all | solution.py:77
  227.8 18.9 %copy-start.8 = (bf16[96,128,32]{1,2,0:T(8,128)(2,1)}, bf16[96,128,32]{1,2,0:T(8,128)(2,1)S(1)}, u32[]{:S(2)}) copy-start(bf16[96,128,32]{1,2,0:T(8,128)(2,1)S(1)} %broadcast_select_fusion) | copy-start | bytes 2359300
  248.6 4.2 copy-start
  293.1 2.9 copy-start.15
  310.7 1.4 copy-start.13
  321.1 1.3 copy-start.14
  346.1 26.7 %all-to-all-start.2 = ((bf16[128,16,128]{2,0,1:T(8,128)(2,1)}), bf16[128,16,128]{2,0,1:T(8,128)(2,1)}, u32[]{:S(2)}, u32[]{:S(2)}) async-start(bf16[128,16,128]{2,0,1:T(8,128)(2,1)} %bitcast.440), calls=%async_computation.2 | async-start | bytes 1048576 | tf_op jit(solution)/shard_map/all_to_all | solution.py:114
  355.4 173.0 %reduce-scatter.2.cloned.1.call-start = ((), (), s32[]{:S(2)}) async-start(), calls=%async_computation.7 | async-start | bytes 3342336 | tf_op jit(solution)/shard_map/reduce_scatter | solution.py:160
  361.0 4.4 copy-start.9
  361.0 5.1 copy-start.22
  361.0 5.1 copy-start.23
  379.6 3.3 copy-start.1
  379.6 3.3 copy-start.6
  393.5 3.6 copy-start.1
  393.5 3.6 copy-start.6
  407.9 3.6 copy-start.1
  407.9 3.6 copy-start.6
  422.4 3.6 copy-start.1
  422.4 3.6 copy-start.6
  436.9 82.3 %copy-start.4 = (f32[6,128,128]{2,1,0:T(8,128)S(1)}, f32[6,128,128]{2,1,0:T(8,128)}, u32[]{:S(2)}) copy-start(f32[6,128,128]{2,1,0:T(8,128)} %copy-done.3) | copy-start | bytes 1179652
  447.6 82.2 %all-to-all-start.3 = ((bf16[2048,3,1,128]{3,1,2,0:T(4,128)(2,1)}), bf16[2048,3,1,128]{3,1,2,0:T(4,128)(2,1)}, u32[]{:S(2)}, u32[]{:S(2)}) async-start(bf16[2048,3,1,128]{3,1,2,0:T(4,128)(2,1)} %copy.299), calls=%async_computation.3 | async-start | bytes 4194304 | tf_op jit(solution)/shard_map/all_to_all | solution.py:157
  457.2 221.9 %all-reduce.2.cloned.1.call-start = ((), (), s32[]{:S(2)}) async-start(), calls=%async_computation.8 | async-start | bytes 393216 | tf_op jit(solution)/shard_map/psum | solution.py:163
  529.8 150.8 %copy-start.7 = (f32[6,1,128,128]{2,3,1,0:T(8,128)S(1)}, f32[6,1,128,128]{2,3,1,0:T(8,128)}, u32[]{:S(2)}) copy-start(f32[6,1,128,128]{2,3,1,0:T(8,128)} %custom-call.28) | copy-start | bytes 1179652
  532.7 148.8 %copy-start.21 = (f32[6,128,128]{2,1,0:T(8,128)S(1)}, f32[6,128,128]{2,1,0:T(8,128)}, u32[]{:S(2)}) copy-start(f32[6,128,128]{2,1,0:T(8,128)} %fusion.52) | copy-start | bytes 1179652
  532.8 149.6 %copy-start.20 = (f32[6,128,128]{2,1,0:T(8,128)S(1)}, f32[6,128,128]{2,1,0:T(8,128)}, u32[]{:S(2)}) copy-start(f32[6,128,128]{2,1,0:T(8,128)} %copy-done.19) | copy-start | bytes 1179652
  532.8 150.5 %copy-start.31 = (pred[128,128]{1,0:T(8,128)(4,1)S(1)}, pred[128,128]{1,0:T(8,128)(4,1)}, u32[]{:S(2)}) copy-start(pred[128,128]{1,0:T(8,128)(4,1)} %copy-done.30) | copy-start | bytes 49156
  680.7 4.0 copy-start.27
  680.7 4.0 copy-start.35
  680.7 4.0 copy-start.38
  682.3 3.2 copy-start.18
  684.7 2.6 copy-start.32
  684.7 2.6 copy-start.33
  684.7 2.6 copy-start.34
  685.6 3.3 copy-start.29
  (5 other events, 5.0 us)
Sparse Core Ops, SparseCore 0:
  144.3 47.7 all-gather.2
  194.0 84.9 all-gather.4
  372.8 68.8 reduce-scatter.1
  528.5 150.6 all-reduce.1
where the time goes:
time: 709 us; the launch traced here: 698 us
  other arithmetic  238 us (34%)
  waiting for transfers between devices  203 us (29%)
  matrix products  119 us (17%)
  local copies, waits for them, and re-layouts  89.3 us (13%)
  starting transfers between devices  34 us (5%)
  between operations  15.3 us (2%)
    psum x1, waiting for transfers between devices, local(): owner_grad = lax.psum(block_share, 'seq').astype(jnp.float32)  144 us
    another operation x3, other arithmetic, cayley(): lax.linalg.triangular_solve(factor_low, halfway, left_side=True, lower=Tr...  120 us
    another operation x3, other arithmetic, cayley(): factor_low = jnp.linalg.cholesky(gram_matrix)  70.5 us
    gather x16, local copies, waits for them, and re-layouts, reorder(): jnp.take(matrix.reshape(row_count, ordering.shape[0], -1), ordering, axis=1)  38.7 us
    all_to_all x1, waiting for transfers between devices, local(): lax.all_to_all(local_rows, 'seq', split_axis=2, concat_axis=0, tiled=True)  35.6 us
    dot_general x1, matrix products, local(): lax.dot_general(upstream, weight_full, (((1,), (1,)), ((), ())), preferre...  17.7 us
    dot_general x4, matrix products, backward_block(): jnp.einsum('qhd,khd->hqk', dout_block, value_rows, preferred_element_type...  15.8 us
    all_to_all x1, waiting for transfers between devices, local(): lax.all_to_all(attended, 'seq', split_axis=0, concat_axis=1, tiled=True)  15.7 us
  transfers between devices with their start and end apart: 8, of which 5 were waited for; matrix products, arithmetic and copies ran while one was open for 33% of the time, Pallas kernels for 0%

commit v1 on v0

--- a/solution.py
+++ b/solution.py
@@ -160,7 +160,7 @@
     block_share = lax.psum_scatter(
         rot_grad.astype(jnp.bfloat16), "fsdp", scatter_dimension=0, tiled=True
     )
-    owner_grad = lax.psum(block_share, "seq").astype(jnp.float32)
+    owner_grad = jnp.sum(lax.all_gather(block_share, "seq"), axis=0).astype(jnp.float32)
     total_tokens = lax.axis_size("fsdp") * length_all
     unused, pullback = jax.vjp(cayley, skew_params)
     grad_skew = pullback(owner_grad * (1.0 / math.sqrt(total_tokens)))[0]

time: 709 us -> 616 us (0.87)
  the two profiles are of different devices: /device:TPU:2 before, /device:TPU:4 now
where the time goes in v1:
time: 616 us; the launch traced here: 605 us
  other arithmetic  248 us (40%)
  matrix products  110 us (18%)
  waiting for transfers between devices  106 us (17%)
  local copies, waits for them, and re-layouts  84.3 us (14%)
  starting transfers between devices  40.8 us (7%)
  between operations  15.2 us (2%)
    another operation x3, other arithmetic, cayley(): lax.linalg.triangular_solve(factor_low, halfway, left_side=True, lower=Tr...  120 us
    another operation x3, other arithmetic, cayley(): factor_low = jnp.linalg.cholesky(gram_matrix)  70.5 us
    reduce_scatter x1, waiting for transfers between devices, local(): lax.psum_scatter(rot_grad.astype(jnp.bfloat16), 'fsdp', scatter_dimension...  51 us
    gather x16, local copies, waits for them, and re-layouts, reorder(): jnp.take(matrix.reshape(row_count, ordering.shape[0], -1), ordering, axis=1)  38.7 us
    all_to_all x1, waiting for transfers between devices, local(): lax.all_to_all(local_rows, 'seq', split_axis=2, concat_axis=0, tiled=True)  32.4 us
    dot_general x4, matrix products, backward_block(): jnp.einsum('qhd,khd->hqk', dout_block, value_rows, preferred_element_type...  15.7 us
    dot_general x4, matrix products, backward_block(): jnp.einsum('hqk,qhd->khd', dscores, query_block, preferred_element_type=j...  13.8 us
    dot_general x4, matrix products, backward_block(): jnp.einsum('hqk,qhd->khd', rounded, dout_block, preferred_element_type=jn...  13.4 us
  transfers between devices with their start and end apart: 8, of which 4 were waited for; matrix products, arithmetic and copies ran while one was open for 36% of the time, Pallas kernels for 0%

profile of v1, /device:TPU:4, one launch (start us, length us, event | category | flops | bytes accessed | tf_op | source)
XLA Modules:
  0.0 605.2 jit_solution(16756028195071688867)
XLA Ops:
  10.6 70.3 %custom-call.23 = f32[6,128,128]{2,1,0:T(8,128)S(1)} custom-call(f32[6,128,128]{2,1,0:T(8,128)S(1)} %fusion.64), custom_call_target="Cholesky" | custom-call | tf_op jit(solution)/shard_map/jit(cholesky)/cholesky/custom-call.1 | solution.py:20
  82.6 58.9 %custom-call.25 = f32[6,1,128,128]{2,3,1,0:T(8,128)S(1)} custom-call(f32[6,1,128,128]{3,2,1,0:T(8,128)S(1)} %get-tuple-element.302), custom_call_target="InvertDiagBlocksLowerTriangular" | custom-call | tf_op jit(solution)/shard_map/triangular_solve/custom-call.0 | solution.py:22
  147.5 11.4 %all-to-all-start = ((bf16[128,3,16,128]{3,0,1,2:T(8,128)(2,1)}), bf16[128,3,16,128]{3,0,1,2:T(8,128)(2,1)S(1)}, u32[]{:S(2)}, u32[]{:S(2)}) async-start(bf16[128,3,16,128]{3,0,1,2:T(8,128)(2,1)} %copy.269), calls=%async_computation | async-start | bytes 3145728 | tf_op jit(solution)/shard_map/all_to_all | solution.py:55
  163.0 32.4 %all-to-all-done = bf16[128,3,16,128]{3,0,1,2:T(8,128)(2,1)S(1)} async-done(((bf16[128,3,16,128]{3,0,1,2:T(8,128)(2,1)}), bf16[128,3,16,128]{3,0,1,2:T(8,128)(2,1)S(1)}, u32[]{:S(2)}, u32[]{:S(2)}) %all-to-all-start) | async-done | bytes 1572896 | tf_op jit(solution)/shard_map/all_to_all | solution.py:55
  195.7 21.3 %while.29 = (s32[]{:T(128)}, bf16[4,512,1,128]{3,1,2,0:T(8,128)(2,1)S(1)}, f32[4,512,1,128]{3,1,2,0:T(8,128)}, bf16[4,1,512,2048]{3,2,1,0:T(8,128)(2,1)}, bf16[4...) while((s32[]{:T(128)}, ...), condition=%wide.region_5.9_spmd, body=%wide.region_2.8_spmd.sunk | while | flops 546372608 | bytes 20982876 | solution.py:75
  219.8 8.0 %all-to-all-start.1 = ((bf16[16,2,8192]{2,1,0:T(2,128)(2,1)}), bf16[16,2,8192]{2,1,0:T(2,128)(2,1)S(1)}, u32[]{:S(2)}, u32[]{:S(2)}) async-start(bf16[16,2,8192]{2,1,0:T(2,128)(2,1)} %reshape.570), calls=%async_computation.1 | async-start | bytes 1048576 | tf_op jit(solution)/shard_map/all_to_all | solution.py:77
  229.3 13.1 %all-to-all-done.1 = bf16[16,2,8192]{2,1,0:T(2,128)(2,1)S(1)} async-done(((bf16[16,2,8192]{2,1,0:T(2,128)(2,1)}), bf16[16,2,8192]{2,1,0:T(2,128)(2,1)S(1)}, u32[]{:S(2)}, u32[]{:S(2)}) %all-to-all-start.1) | async-done | bytes 524320 | tf_op jit(solution)/shard_map/all_to_all | solution.py:77
  247.4 2.9 gather_fusion.10
  252.8 2.7 gather_fusion.11
  257.9 2.7 gather_fusion.12
  263.2 2.7 gather_fusion.13
  268.1 2.8 gather_fusion.14
  270.9 8.8 %all-gather.7.cloned.1.call-done = bf16[2048,3072]{1,0:T(8,128)(2,1)} async-done(((bf16[128,3072]{1,0:T(8,128)(2,1)}), bf16[2048,3072]{1,0:T(8,128)(2,1)}) %all-gather.7.cloned.1.call-update) | async-done | bytes 12582928 | tf_op jit(solution)/shard_map/all_gather | solution.py:49
  279.7 7.5 %convolution_convert_fusion.1 = bf16[128,3072]{1,0:T(8,128)(2,1)} fusion(bf16[128,2048]{0,1:T(8,128)(2,1)} %bitcast.440, bf16[2048,3072]{1,0:T(8,128)(2,1)} %all-gather.7.cloned.1.call-done), kind=kOutput, calls=%fused_computation.60 | convolution fusion | flops 1611005952 | bytes 13893632 | tf_op jit(solution)/shard_map/dot_general | solution.py:80
  289.5 2.7 gather_fusion
  296.7 2.7 gather_fusion.1
  301.8 2.7 gather_fusion.15
  304.5 2.9 bitcast_convert_fusion.1
  307.4 2.7 gather_fusion.2
  311.4 2.7 fusion.29
  315.4 2.7 gather_fusion.3
  320.4 2.7 gather_fusion.4
  324.4 2.7 fusion.30
  328.4 2.7 gather_fusion.5
  333.4 2.7 gather_fusion.6
  340.3 10.2 %pad_maximum_fusion = bf16[4,24,128,128]{3,2,1,0:T(8,128)(2,1)} fusion(bf16[1,24,128,128]{3,2,1,0:T(8,128)(2,1)S(1)} %fusion.31, bf16[1,24,128,128]{3,2,1,0:T(8,128)(2,1)S(1)} %copy-done.21, bf16[1,24,128,128]{3,2,1,0:T(8,128)(2,1)S(1)} %copy-done.20, bf16[1,24,128,128]{3,2,1,0:T(8,128)(2,1)S(1)} %copy-done.19), kind=kLoop, calls=%fused_computation.61 | loop fusion | flops 4718592 | bytes 6291456 | tf_op jit(solution)/shard_map/stack | solution.py:110
  350.5 9.1 %fusion.32 = bf16[16,16,8,128]{3,2,1,0:T(8,128)(2,1)S(1)} fusion(bf16[128,3072]{0,1:T(8,128)(2,1)} %bitcast.439, bf16[2048,3072]{1,0:T(8,128)(2,1)} %all-gather.7.cloned.1.call-done), kind=kOutput, calls=%fused_computation.80 | convolution fusion | flops 1610874880 | bytes 13893632 | tf_op jit(solution)/shard_map/dot_general | solution.py:111
  360.6 10.0 %all-to-all-start.2 = ((bf16[128,16,128]{2,0,1:T(8,128)(2,1)}), bf16[128,16,128]{2,0,1:T(8,128)(2,1)}, u32[]{:S(2)}, u32[]{:S(2)}) async-start(bf16[128,16,128]{2,0,1:T(8,128)(2,1)} %bitcast.442), calls=%async_computation.2 | async-start | bytes 1048576 | tf_op jit(solution)/shard_map/all_to_all | solution.py:114
  370.6 51.0 %reduce-scatter.2.cloned.1.call-done = bf16[6,128,128]{2,1,0:T(8,128)(2,1)} async-done(((bf16[96,128,128]{2,1,0:T(8,128)(2,1)}), bf16[6,128,128]{2,1,0:T(8,128)(2,1)}) %reduce-scatter.2.cloned.1.call-update) | async-done | bytes 196624 | tf_op jit(solution)/shard_map/reduce_scatter | solution.py:160
  422.6 56.6 %while.30 = (s32[]{:T(128)}, f32[2048,1,128]{0,2,1:T(8,128)}, f32[2048,1,128]{0,2,1:T(8,128)}, bf16[4,512,1,128]{3,1,2,0:T(8,128)(2,1)}, bf16[4,512,1,128]{3,1,2...) while((s32[]{:T(128)}, f32[2048,1,128]{0,2,1:T(8,128)}, ...), condition=%wide.region_11.17_spmd.clone, body=%wide.region_10.16_spmd.clone.sunk | while | flops 1080294912 | bytes 27663552 | solution.py:143
  424.6 3.9 multiply_convert_fusion.2
  428.5 3.2 fusion.189
  433.2 3.1 fusion.190
  438.3 3.9 multiply_convert_fusion.2
  442.3 3.5 fusion.189
  447.2 3.4 fusion.190
  452.6 3.9 multiply_convert_fusion.2
  456.6 3.5 fusion.189
  461.5 3.4 fusion.190
  466.9 3.9 multiply_convert_fusion.2
  470.8 3.5 fusion.189
  475.7 3.4 fusion.190
  485.1 10.7 %copy.294 = bf16[2048,3,1,128]{3,1,2,0:T(4,128)(2,1)} copy(bf16[2048,3,1,128]{3,0,1,2:T(8,128)(2,1)S(1)} %maximum_bitcast_fusion) | data formatting | bytes 3145728 | tf_op jit(solution)/shard_map/reshape | solution.py:156
  495.9 11.2 %all-to-all-start.3 = ((bf16[2048,3,1,128]{3,1,2,0:T(4,128)(2,1)}), bf16[2048,3,1,128]{3,1,2,0:T(4,128)(2,1)}, u32[]{:S(2)}, u32[]{:S(2)}) async-start(bf16[2048,3,1,128]{3,1,2,0:T(4,128)(2,1)} %copy.294), calls=%async_computation.3 | async-start | bytes 4194304 | tf_op jit(solution)/shard_map/all_to_all | solution.py:157
  507.0 60.4 %custom-call.28 = f32[6,1,128,128]{2,3,1,0:T(8,128)} custom-call(f32[6,1,128,128]{3,2,1,0:T(8,128)} %get-tuple-element.301), custom_call_target="InvertDiagBlocksLowerTriangular" | custom-call | tf_op jit(solution)/shard_map/transpose(jvp())/triangular_solve/custom-call.3 | solution.py:22
  573.5 2.5 fusion.108
  579.2 2.9 copy.295
  584.2 2.6 reduce_sum.21
  (238 shorter events, 122.3 us)
Async XLA Ops:
  7.2 236.9 %all-gather.5.cloned.1.call-start = ((), (), s32[]{:S(2)}) async-start(), calls=%async_computation.5 | async-start | bytes 3342336 | tf_op jit(solution)/shard_map/all_gather | solution.py:51
  7.2 135.7 %copy-start.22 = (f32[128,128]{1,0:T(8,128)}, f32[128,128]{1,0:T(8,128)S(1)}, u32[]{:S(2)}) copy-start(f32[128,128]{1,0:T(8,128)S(1)} %get-tuple-element.320) | copy-start | bytes 196612
  9.5 133.5 %copy-start.3 = (f32[6,128,128]{2,1,0:T(8,128)}, f32[6,128,128]{2,1,0:T(8,128)S(1)}, u32[]{:S(2)}) copy-start(f32[6,128,128]{2,1,0:T(8,128)S(1)} %bitcast_subtract_fusion) | copy-start | bytes 1179652
  10.5 134.5 %copy-start.24 = (bf16[1,128,3,2048]{3,1,2,0:T(8,128)(2,1)S(1)}, bf16[1,128,3,2048]{3,1,2,0:T(8,128)(2,1)}, u32[]{:S(2)}) copy-start(bf16[1,128,3,2048]{3,1,2,0:T(8,128)(2,1)} %param.18) | copy-start | bytes 4718596
  80.9 1.7 copy-start.25
  81.1 63.2 %copy-start.35 = (pred[6]{0:T(512)(128)(4,1)}, pred[6]{0:T(512)(128)(4,1)S(1)}, u32[]{:S(2)}) copy-start(pred[6]{0:T(512)(128)(4,1)S(1)} %compare_reduce_fusion) | copy-start | bytes 22
  141.6 2.7 copy-start.14
  144.2 135.5 %all-gather.7.cloned.1.call-start = ((), (), s32[]{:S(2)}) async-start(), calls=%async_computation.6 | async-start | bytes 13369344 | tf_op jit(solution)/shard_map/all_gather | solution.py:49
  145.9 13.0 %copy-start.34 = (s32[4,96]{1,0:T(4,128)S(1)}, s32[4,96]{1,0:T(4,128)}, u32[]{:S(2)}) copy-start(s32[4,96]{1,0:T(4,128)} %param.21) | copy-start | bytes 4612
  147.5 47.9 %all-to-all-start = ((bf16[128,3,16,128]{3,0,1,2:T(8,128)(2,1)}), bf16[128,3,16,128]{3,0,1,2:T(8,128)(2,1)S(1)}, u32[]{:S(2)}, u32[]{:S(2)}) async-start(bf16[128,3,16,128]{3,0,1,2:T(8,128)(2,1)} %copy.269), calls=%async_computation | async-start | bytes 3145728 | tf_op jit(solution)/shard_map/all_to_all | solution.py:55
  217.1 10.8 %copy-start.13 = (bf16[4,512,1,128]{3,1,2,0:T(8,128)(2,1)}, bf16[4,512,1,128]{3,1,2,0:T(8,128)(2,1)S(1)}, u32[]{:S(2)}) copy-start(bf16[4,512,1,128]{3,1,2,0:T(8,128)(2,1)S(1)} %get-tuple-element.514) | copy-start | bytes 1572868
  217.1 11.2 %copy-start.5 = (bf16[2048,1,128]{2,0,1:T(8,128)(2,1)}, bf16[2048,1,128]{2,0,1:T(8,128)(2,1)S(1)}, u32[]{:S(2)}) copy-start(bf16[2048,1,128]{2,0,1:T(8,128)(2,1)S(1)} %get-tuple-element.509) | copy-start | bytes 1572868
  217.1 12.0 %copy-start.2 = (bf16[2048,1,128]{2,0,1:T(8,128)(2,1)}, bf16[2048,1,128]{2,0,1:T(8,128)(2,1)S(1)}, u32[]{:S(2)}) copy-start(bf16[2048,1,128]{2,0,1:T(8,128)(2,1)S(1)} %get-tuple-element.508) | copy-start | bytes 1572868
  217.1 10.8 %copy-start.27 = (bf16[1,128,3072]{2,1,0:T(8,128)(2,1)S(1)}, bf16[1,128,3072]{2,1,0:T(8,128)(2,1)}, u32[]{:S(2)}) copy-start(bf16[1,128,3072]{2,1,0:T(8,128)(2,1)} %param.22) | copy-start | bytes 2359300
  219.8 22.6 %all-to-all-start.1 = ((bf16[16,2,8192]{2,1,0:T(2,128)(2,1)}), bf16[16,2,8192]{2,1,0:T(2,128)(2,1)S(1)}, u32[]{:S(2)}, u32[]{:S(2)}) async-start(bf16[16,2,8192]{2,1,0:T(2,128)(2,1)} %reshape.570), calls=%async_computation.1 | async-start | bytes 1048576 | tf_op jit(solution)/shard_map/all_to_all | solution.py:77
  227.9 193.8 %reduce-scatter.2.cloned.1.call-start = ((), (), s32[]{:S(2)}) async-start(), calls=%async_computation.7 | async-start | bytes 3342336 | tf_op jit(solution)/shard_map/reduce_scatter | solution.py:160
  229.3 16.3 %copy-start.9 = (bf16[96,128,32]{1,2,0:T(8,128)(2,1)}, bf16[96,128,32]{1,2,0:T(8,128)(2,1)S(1)}, u32[]{:S(2)}) copy-start(bf16[96,128,32]{1,2,0:T(8,128)(2,1)S(1)} %broadcast_select_fusion) | copy-start | bytes 2359300
  247.4 4.2 copy-start
  251.6 1.3 copy-start.10
  261.9 1.3 copy-start.11
  293.8 2.9 copy-start.12
  336.1 4.2 copy-start.19
  336.1 4.2 copy-start.20
  336.1 4.2 copy-start.21
  360.6 61.1 %all-to-all-start.2 = ((bf16[128,16,128]{2,0,1:T(8,128)(2,1)}), bf16[128,16,128]{2,0,1:T(8,128)(2,1)}, u32[]{:S(2)}, u32[]{:S(2)}) async-start(bf16[128,16,128]{2,0,1:T(8,128)(2,1)} %bitcast.442), calls=%async_computation.2 | async-start | bytes 1048576 | tf_op jit(solution)/shard_map/all_to_all | solution.py:114
  370.6 213.6 %all-gather.9.cloned.1.call-start = ((), (), s32[]{:S(2)}) async-start(), calls=%async_computation.8 | async-start | bytes 3342336 | tf_op jit(solution)/shard_map/all_gather | solution.py:163
  428.5 3.3 copy-start.1
  428.5 3.3 copy-start.6
  442.3 3.5 copy-start.1
  442.3 3.5 copy-start.6
  456.6 3.5 copy-start.1
  456.6 3.5 copy-start.6
  470.8 3.5 copy-start.1
  470.8 3.5 copy-start.6
  485.1 83.6 %copy-start.4 = (f32[6,128,128]{2,1,0:T(8,128)S(1)}, f32[6,128,128]{2,1,0:T(8,128)}, u32[]{:S(2)}) copy-start(f32[6,128,128]{2,1,0:T(8,128)} %copy-done.3) | copy-start | bytes 1179652
  495.9 83.4 %all-to-all-start.3 = ((bf16[2048,3,1,128]{3,1,2,0:T(4,128)(2,1)}), bf16[2048,3,1,128]{3,1,2,0:T(4,128)(2,1)}, u32[]{:S(2)}, u32[]{:S(2)}) async-start(bf16[2048,3,1,128]{3,1,2,0:T(4,128)(2,1)} %copy.294), calls=%async_computation.3 | async-start | bytes 4194304 | tf_op jit(solution)/shard_map/all_to_all | solution.py:157
  582.1 4.7 copy-start.23
  582.1 5.5 copy-start.18
  584.2 5.2 copy-start.7
  584.2 6.0 copy-start.17
  586.8 4.4 copy-start.29
  588.5 4.0 copy-start.26
  588.5 4.0 copy-start.33
  588.6 4.0 copy-start.36
  590.2 3.3 copy-start.15
  592.5 2.6 copy-start.30
  592.5 2.6 copy-start.31
  592.6 2.6 copy-start.32
  (3 other events, 2.6 us)
Sparse Core Ops, SparseCore 0:
  144.4 48.2 all-gather.4
  194.5 85.2 all-gather.6
  350.7 70.9 reduce-scatter.1
  424.1 104.4 all-gather.8
